TPU v7x, 512 devices: a whole 4x8x8 slice. The times are simulated.
512 devices in a mesh: dp: 32 (over y_hi, z, core), tp: 16 (over y_lo, x).
Axes of the slice: x: 4, y: 8 (y_hi: 2, y_lo: 4; y = y_hi * 4 + y_lo), z: 8, core: 2. Of those that a mesh axis runs over, the one named last changes fastest.
Arguments:
- q_latent: bfloat16 [1024, 128, 576], P(('dp', 'tp')), may hold values from -160 to 160
- page_pool: bfloat16 [16384, 64, 576], P(('dp', 'tp')), may hold values from -6 to 6
- block_table: int32 [1024, 16], P(('dp', 'tp')), may hold values from 0 to 31, as said below
- cache_len: int32 [1024], P(('dp', 'tp')), may hold values from 1 to 1024
- prompt_of_row: int32 [1024], P(('dp', 'tp')), may hold values from 0 to 7
- prefix_cache: bfloat16 [32, 1024, 576], P('dp', 'tp'), may hold values from -6 to 6
- prefix_pages: int32 [8], replicated, may hold values from 1 to 16
- owners: int32 [8], replicated, may hold values from 0 to 31, as said below
Outputs:
- attended: bfloat16 [1024, 128, 512], P(('dp', 'tp'))
Inputs may be any that keep to these rules, and one draw needn't show every extreme that they name: `block_table`: each device's rows name its own pages: the entries of its 2 rows together are every number below 32 once. `owners`: distinct ranks.
All inputs are finite; a program needn't handle non-finite values.
Results may differ from a plain program's by a relative error of at most 0.009.
Values may be sent and summed in bfloat16 or wider, within the bound.
A program may use at most 64 MiB of HBM per device.

v0:
```python
import jax
import jax.numpy as jnp
from jax import lax
from jax.sharding import PartitionSpec as P

LAT = 512


score_scale = 192.0 ** (-0.5)
big_negative = -1e30


def broadcast(x, axis, root):
    mine = lax.axis_index(axis) == root
    return lax.psum(jnp.where(mine, x, jnp.zeros_like(x)), axis)


def attend(state, queries, keys, valid):
    running, total, numerator = state
    latent = numerator.shape[-1]
    score = jnp.einsum("rhk,rtk->rht", queries, keys, preferred_element_type=jnp.float32)
    values = keys[:, :, :latent]
    score = jnp.where(valid[:, None, :], score * score_scale, big_negative)
    newest = jnp.maximum(running, jnp.max(score, axis=-1))
    rescale = jnp.exp(running - newest)
    weight = jnp.where(valid[:, None, :], jnp.exp(score - newest[..., None]), 0.0)
    total = rescale * total + jnp.sum(weight, axis=-1)
    added = jnp.einsum(
        "rht,rtv->rhv", weight.astype(jnp.bfloat16), values, preferred_element_type=jnp.float32
    )
    numerator = rescale[..., None] * numerator + added
    return (newest, total, numerator)


def empty_state(rows, heads, latent):
    return (
        jnp.full((rows, heads), big_negative, jnp.float32),
        jnp.zeros((rows, heads), jnp.float32),
        jnp.zeros((rows, heads, latent), jnp.float32),
    )


def on_device(
    q_latent, page_pool, block_table, cache_len, prompt_of_row, prefix_cache, prefix_pages, owners
):
    rows_dev, max_pages = block_table.shape
    page_tokens = page_pool.shape[1]
    width = page_pool.shape[2]
    heads = q_latent.shape[1]
    latent = LAT
    block_pages = min(max_pages, 8)
    span = block_pages * page_tokens
    state = empty_state(rows_dev, heads, latent)
    blocks = (jnp.max(cache_len) + span - 1) // span

    def private_step(index, carry):
        pages = lax.dynamic_slice_in_dim(block_table, index * block_pages, block_pages, 1)
        keys = page_pool[pages].reshape(rows_dev, span, width)
        where_at = index * span + jnp.arange(span, dtype=jnp.int32)
        valid = where_at[None, :] < cache_len[:, None]
        return attend(carry, q_latent, keys, valid)

    state = lax.fori_loop(0, blocks, private_step, state)
    prompts = owners.shape[0]
    pieces = [broadcast(prefix_cache, "dp", owners[number]) for number in range(prompts)]
    prefix = jnp.concatenate(pieces, 0)
    limits = prefix_pages * page_tokens
    row_limits = limits[prompt_of_row]
    piece = lax.all_gather(prefix, "tp", axis=1, tiled=True)
    count = piece.shape[1]
    tokens = jnp.arange(count, dtype=jnp.int32)
    valid = tokens[None, :] < row_limits[:, None]
    keys = piece[prompt_of_row]
    state = attend(state, q_latent, keys, valid)
    running, total, numerator = state
    return (numerator / total[..., None]).astype(jnp.bfloat16)


def solution(mesh):
    placed = (
        P(("dp", "tp"), None, None),
        P(("dp", "tp"), None, None),
        P(("dp", "tp"), None),
        P(("dp", "tp")),
        P(("dp", "tp")),
        P("dp", "tp", None),
        P(),
        P(),
    )
    return jax.shard_map(
        on_device,
        mesh=mesh,
        in_specs=placed,
        out_specs=P(("dp", "tp"), None, None),
        check_vma=False,
    )
```

profile of v0, /device:TPU:1, one launch (start us, length us, event | category | flops | bytes accessed | tf_op | source)
XLA Modules:
  0.0 505.1 jit_solution(9219533324492811002)
XLA Ops:
  6.5 0.0 copy-start.2
  6.5 0.0 copy-start.4
  6.5 0.0 copy-start.5
  6.5 0.0 copy-start.3
  6.5 0.0 copy-start.1
  6.5 0.0 all-reduce.3.cloned.1.call-start
  6.6 1.6 fusion.31
  13.2 1.7 broadcast_select_fusion
  15.0 0.0 all-reduce.3.cloned.1.call-update
  15.0 0.0 all-gather.2.cloned.1.call-start
  15.0 344.1 %all-reduce.3.cloned.1.call-done = (bf16[1,64,576]{2,1,0:T(8,128)(2,1)}, bf16[1,64,576]{2,1,0:T(8,128)(2,1)}, bf16[1,64,576]{2,1,0:T(8,128)(2,1)}, bf16[1,64,576...) async-done(((bf16[1,64,576]{2,1,0:T(8,128)(2,1)}, ...) | async-done | bytes 589840 | tf_op jit(solution)/shard_map/psum | solution.py:15
  359.1 0.9 constant_dynamic-update-slice_fusion.7
  360.0 0.9 constant_dynamic-update-slice_fusion.6
  360.9 0.9 constant_dynamic-update-slice_fusion.5
  361.8 0.9 constant_dynamic-update-slice_fusion.4
  362.7 0.9 constant_dynamic-update-slice_fusion.3
  363.6 0.9 constant_dynamic-update-slice_fusion.2
  364.5 0.9 constant_dynamic-update-slice_fusion.1
  365.4 0.9 constant_dynamic-update-slice_fusion
  366.3 0.0 copy-start
  366.3 0.8 copy-done
  367.2 0.0 all-gather.2.cloned.1.call-update
  367.2 0.0 copy-done.2
  367.2 0.6 reduce_max.27
  368.5 0.0 copy-done.4
  368.5 0.0 copy-done.5
  368.6 0.6 gather_fusion.1
  369.2 0.1 iota_compare_fusion
  369.3 0.1 broadcast_in_dim.71
  369.3 0.0 copy-done.3
  369.4 0.0 copy-done.1
  369.4 8.7 %while.14 = (s32[]{:T(128)}, f32[2,128]{1,0:T(2,128)S(1)}, f32[2,128]{1,0:T(2,128)S(1)}, f32[2,128,512]{2,1,0:T(8,128)S(1)}, s32[]{:T(128)}, /*index=5*/s32[2]{0...) while((s32[]{:T(128)}, f32[2,128]{1,0:T(2,128)S(1)}, ...), condition=%wide.region_4.5_spmd, body=%wide.region_1.4_spmd.sunk | while | flops 286657600 | bytes 7534159 | solution.py:63
  369.4 0.1 compare_select_fusion.3
  369.5 0.1 reshape.86
  369.6 2.5 gather_fusion
  372.1 0.1 broadcast_compare_fusion.2
  372.2 0.5 fusion.47
  372.7 0.2 fusion.48
  372.9 0.7 convolution_add_fusion.2
  373.7 0.1 compare_select_fusion.3
  373.8 0.1 reshape.86
  373.9 2.5 gather_fusion
  376.4 0.1 broadcast_compare_fusion.2
  376.5 0.5 fusion.47
  377.0 0.2 fusion.48
  377.3 0.7 convolution_add_fusion.2
  378.1 111.9 %all-gather.2.cloned.1.call-done = bf16[8,1024,576]{2,1,0:T(8,128)(2,1)} async-done(((bf16[8,64,576]{2,1,0:T(8,128)(2,1)}), bf16[8,1024,576]{2,1,0:T(8,128)(2,1)}) %all-gather.2.cloned.1.call-update) | async-done | bytes 9437200 | tf_op jit(solution)/shard_map/all_gather | solution.py:69
  490.0 5.0 gather_fusion.2
  495.0 1.1 fusion.32
  496.1 0.3 fusion.23
  496.5 1.8 fusion.20
  (17 shorter events, 0.1 us)
Async XLA Ops:
  6.5 360.7 %copy-start.2 = (s32[2]{0:T(128)S(1)}, s32[2]{0:T(128)}, u32[]{:S(2)}) copy-start(s32[2]{0:T(128)} %param.13) | copy-start | bytes 28
  6.5 362.0 %copy-start.4 = (s32[2]{0:T(128)S(1)}, s32[2]{0:T(128)}, u32[]{:S(2)}) copy-start(s32[2]{0:T(128)} %param.14) | copy-start | bytes 28
  6.5 362.0 %copy-start.5 = (s32[8]{0:T(128)S(1)}, s32[8]{0:T(128)}, u32[]{:S(2)}) copy-start(s32[8]{0:T(128)} %param.16) | copy-start | bytes 100
  6.5 362.8 %copy-start.3 = (bf16[2,128,576]{1,2,0:T(8,128)(2,1)S(1)}, bf16[2,128,576]{1,2,0:T(8,128)(2,1)}, u32[]{:S(2)}) copy-start(bf16[2,128,576]{1,2,0:T(8,128)(2,1)} %param.10) | copy-start | bytes 884740
  6.5 362.8 %copy-start.1 = (s32[2,16]{1,0:T(2,128)S(1)}, s32[2,16]{1,0:T(2,128)}, u32[]{:S(2)}) copy-start(s32[2,16]{1,0:T(2,128)} %param.12) | copy-start | bytes 388
  6.5 352.6 %all-reduce.3.cloned.1.call-start = ((), (), s32[]{:S(2)}) async-start(), calls=%async_computation.1 | async-start | bytes 1310720 | tf_op jit(solution)/shard_map/psum | solution.py:15
  15.0 475.0 %all-gather.2.cloned.1.call-start = ((), (), s32[]{:S(2)}) async-start(), calls=%async_computation | async-start | bytes 11141120 | tf_op jit(solution)/shard_map/all_gather | solution.py:69
  366.3 0.8 copy-start
Sparse Core Ops, SparseCore 0:
  15.1 343.9 all-reduce.2
  367.3 122.6 all-gather.1
where the time goes:
time: 506 us; the launch traced here: 505 us
  waiting for transfers between devices  456 us (90%)
  local copies, waits for them, and re-layouts  20.6 us (4%)
  between operations  19.2 us (4%)
  matrix products  5.41 us (1%)
    psum x1, waiting for transfers between devices, broadcast(): return lax.psum(jnp.where(mine, x, jnp.zeros_like(x)), axis)  344 us
    all_gather x1, waiting for transfers between devices, on_device(): piece = lax.all_gather(prefix, 'tp', axis=1, tiled=True)  112 us
  transfers between devices with their start and end apart: 2, of which 2 were waited for; matrix products, arithmetic and copies ran while one was open for 2% of the time, Pallas kernels for 0%

commit v1 on v0

v1 whole, which is shorter than its diff:
```python
import jax
import jax.numpy as jnp
from jax import lax
from jax.experimental import pallas as pl
from jax.experimental.pallas import tpu as pltpu
from jax.sharding import PartitionSpec as P

LAT = 512
ROPE = 64
WIDTH = LAT + ROPE
HEADS = 128
PAGE = 64
MAXP = 16
PROMPTS = 8
ROWS_DEV = 2
X, Y, Z, DP, TP = 4, 4, 8, 32, 16
NEAR = 2 * Z
POS = PROMPTS + 1
SCALE = 192.0 ** (-0.5)
BIG_NEGATIVE = -1e30
MESH = pl.DeviceIdType.MESH
TN = (((0,), (0,)), ((), ()))
NN = (((1,), (0,)), ((), ()))


def kernel(
    table_hbm, length_hbm, prompt_hbm, pages_hbm, owners_hbm, queries_hbm, slot_hbm, pool_hbm, out,
    table, length, prompt, pages, owners, queries, slot, gathered, received, picked, traded, staged, pool, others, other_block,
    other_prompt, partial, arrived, numer, stats,
    local_sem, prompt_sem, p1_send, p1_recv, z_send, z_recv, t_send, t_recv, r_send, r_recv, c_send, c_recv,
):
    dp = lax.axis_index("dp")
    tp = lax.axis_index("tp")
    core = dp % 2
    z = (dp // 2) % Z
    y_hi = dp // (2 * Z)
    y_lo = tp // X
    x = tp % X
    twin = (dp + 1 - 2 * core, tp)

    def at_y(step):
        y = (y_hi * Y + y_lo + step + 2 * Y) % (2 * Y)
        return (((y // Y) * Z + z) * 2 + core, (y % Y) * X + x)

    def at_x(step):
        return (dp, y_lo * X + (x + step + X) % X)

    def at_z(step):
        return ((y_hi * Z + (z + step + Z) % Z) * 2 + core, tp)

    slot_copy, query_in, pool_copy, *small_copies = [
        pltpu.make_async_copy(source, target, local_sem.at[i])
        for i, (source, target) in enumerate((
            (slot_hbm, slot), (queries_hbm, queries), (pool_hbm, pool), (owners_hbm, owners),
            (prompt_hbm, prompt), (pages_hbm, pages), (table_hbm, table), (length_hbm, length),
        ))
    ]
    for copy in [slot_copy, query_in, pool_copy] + small_copies:
        copy.start()

    barrier = pltpu.get_barrier_semaphore()

    def near(i):
        return y_hi * NEAR + (dp + i) % NEAR

    partner = ((1 - y_hi) * NEAR + dp % NEAR, tp)

    @pl.loop(1, NEAR)
    def _(i):
        pl.semaphore_signal(barrier, inc=1, device_id=(near(i), tp), device_id_type=MESH)

    pl.semaphore_signal(barrier, inc=1, device_id=partner, device_id_type=MESH)

    @pl.loop(1, TP)
    def _(i):
        pl.semaphore_signal(barrier, inc=1, device_id=(dp, (tp + i) % TP), device_id_type=MESH)

    for step in (1, -1):
        pl.semaphore_signal(barrier, inc=1, device_id=at_y(step), device_id_type=MESH)

    slot_copy.wait()

    for half in range(2):
        low = slot[0, 32 * half : 32 * half + 16, LAT:WIDTH]
        high = slot[0, 32 * half + 16 : 32 * half + 32, LAT:WIDTH]
        rotary = jnp.concatenate([low, high], axis=1)
        for tile in range(Z):
            lanes, tokens = tile // 2, tile % 2
            first = 32 * half + 16 * tokens
            staged[half, tile, 0] = slot[0, first : first + 16, 128 * lanes : 128 * lanes + 128]
            staged[half, tile, 1] = rotary

    pl.semaphore_wait(barrier, NEAR - 1 + 1 + TP - 1 + 2)

    def remote(src, dst, send, recv, device):
        return pltpu.make_async_remote_copy(
            src_ref=src, dst_ref=dst, send_sem=send, recv_sem=recv, device_id=device, device_id_type=MESH
        )

    def spread(i):
        to = near(i)
        return remote(
            staged.at[to % 2, (to // 2) % Z], received.at[dp % NEAR], p1_send.at[i], p1_recv.at[i], (to, tp)
        )

    def spread_in(i):
        source = (dp - i + DP) % NEAR
        return remote(
            staged.at[0, 0], received.at[source], p1_send.at[i], p1_recv.at[i], (near(i), tp)
        )

    @pl.loop(1, NEAR)
    def _(i):
        spread(i).start()

    received[dp % NEAR] = staged[core, z]
    prompt_copy = remote(prompt_hbm, other_block, c_send.at[0], c_recv.at[0], twin)
    prompt_copy.start()
    query_copy = remote(queries_hbm, others, c_send.at[1], c_recv.at[1], twin)
    query_copy.start()
    for copy in [query_in] + small_copies:
        copy.wait()

    token = lax.broadcasted_iota(jnp.int32, (4 * PAGE, HEADS), 0)

    def turned_wide(line):
        return jnp.transpose(jnp.broadcast_to(line, (HEADS, HEADS)))

    def attend(scores, values):
        peak = jnp.max(scores[0], axis=0, keepdims=True)
        for score in scores[1:]:
            peak = jnp.maximum(peak, jnp.max(score, axis=0, keepdims=True))
        total = jnp.zeros((1, HEADS), jnp.float32)
        numerator = jnp.zeros((HEADS, LAT), jnp.float32)
        for score, value in zip(scores, values):
            weight = jnp.exp(score - peak)
            total = total + jnp.sum(weight, axis=0, keepdims=True)
            numerator = numerator + lax.dot_general(
                weight.astype(jnp.bfloat16), value(), TN, preferred_element_type=jnp.float32
            )
        return turned_wide(peak), turned_wide(total), numerator

    def private(row):
        limit = length[row]

        def block(number):
            return jnp.concatenate([pool[table[row, 4 * number + i]] for i in range(4)], axis=0)

        scores = []
        for number in range(4):
            score = lax.dot_general(block(number), queries[row], NN, preferred_element_type=jnp.float32)
            scores.append(jnp.where(token + 256 * number < limit, score * SCALE, BIG_NEGATIVE))
        peak, total, numerator = attend(
            scores, [lambda number=number: block(number)[:, :LAT] for number in range(4)]
        )
        numer[row] = numerator
        stats[row, 0] = peak
        stats[row, 1] = total

    pool_copy.wait()
    for row in range(ROWS_DEV):
        private(row)

    @pl.loop(1, NEAR)
    def _(i):
        spread_in(i).wait_recv()

    for p in range(PROMPTS):
        picked[p] = received[owners[p] % NEAR, 0]
    picked[PROMPTS] = received[owners[z] % NEAR, 1]
    trade = remote(picked, traded, c_send.at[4], c_recv.at[4], partner)
    trade.start()
    trade.wait_recv()
    for p in range(POS):
        owner = owners[p] if p < PROMPTS else owners[z]
        gathered[y_lo, x, z, p] = jnp.where(owner // NEAR == y_hi, picked[p], traded[p])

    def z_out(i):
        mine = gathered.at[y_lo, x, z, 0:6]
        return remote(mine, mine, z_send.at[i], z_recv.at[i], at_z(i))

    def z_in(i):
        theirs = gathered.at[y_lo, x, (z - i + Z) % Z, 0:6]
        return remote(theirs, theirs, z_send.at[i], z_recv.at[i], at_z(i))

    def t_out(i):
        mine = gathered.at[y_lo, x, z, 6:9]
        return remote(mine, mine, t_send.at[i], t_recv.at[i], (dp, (tp + i) % TP))

    def t_in(i):
        source = (tp - i + TP) % TP
        theirs = gathered.at[source // X, source % X, z, 6:9]
        return remote(theirs, theirs, t_send.at[i], t_recv.at[i], (dp, (tp + i) % TP))

    @pl.loop(1, Z)
    def _(i):
        z_out(i).start()

    @pl.loop(1, TP)
    def _(i):
        t_out(i).start()

    prompt_copy.wait_recv()
    to_scalar = pltpu.make_async_copy(other_block, other_prompt, prompt_sem)
    to_scalar.start()
    to_scalar.wait()

    started = []

    class Ring:
        def __init__(self, half, place, device, first, size, steps):
            self.half, self.place, self.device = half, place, device
            self.first, self.size, self.steps = first, size, steps

        def copy(self, step, number, way, behind):
            sign = 1 - 2 * way
            origin = (self.place - sign * behind + 2 * self.size) % self.size
            ref = self.half(origin, number if way == 0 else 1 - number)
            index = self.first + 2 * (2 * (step - 1) + number) + way
            return remote(ref, ref, r_send.at[index], r_recv.at[index], self.device(sign))

        def send(self, step, number):
            for way in range(2):
                copy = self.copy(step, number, way, step - 1)
                copy.start()
                started.append(copy)

        def begin(self):
            self.send(1, 0)
            self.send(1, 1)

        def land(self, step, number):
            forward = step + 1 < self.steps or (step + 1 == self.steps and number == 0)
            for way in range(2):
                self.copy(step, number, way, step).wait_recv()
                if forward:
                    copy = self.copy(step + 1, number, way, step)
                    copy.start()
                    started.append(copy)

    ay = Ring(lambda y, h: gathered.at[y, x, 4 * h : 4 * h + 4, 0:3], y_lo, at_y, 0, Y, 2)
    bx = Ring(lambda at, h: gathered.at[y_lo, at, 4 * h : 4 * h + 4, 3:6], x, at_x, 6, X, 2)
    ax = Ring(lambda at, h: gathered.at[2 * h : 2 * h + 2, at, :, 0:3], x, at_x, 12, X, 2)
    by = Ring(lambda y, h: gathered.at[y, 2 * h : 2 * h + 2, :, 3:6], y_lo, at_y, 18, Y, 2)
    cz = Ring(lambda at, h: gathered.at[2 * h : 2 * h + 2, :, at, 6:9], z, at_z, 24, Z, 4)

    @pl.loop(1, Z)
    def _(i):
        z_in(i).wait_recv()

    ay.begin()
    bx.begin()

    @pl.loop(1, TP)
    def _(i):
        t_in(i).wait_recv()

    cz.begin()
    ay.land(1, 0)
    bx.land(1, 0)
    ay.land(1, 1)
    bx.land(1, 1)
    cz.land(1, 0)
    ay.land(2, 0)
    ax.begin()
    bx.land(2, 0)
    by.begin()
    cz.land(1, 1)
    cz.land(2, 0)
    ax.land(1, 0)
    by.land(1, 0)
    cz.land(2, 1)
    cz.land(3, 0)
    ax.land(1, 1)
    by.land(1, 1)
    query_copy.wait_recv()
    cz.land(3, 1)
    cz.land(4, 0)
    ax.land(2, 0)
    by.land(2, 0)

    page_of = lax.broadcasted_iota(jnp.int32, (256, HEADS), 0) // 16
    blank = jnp.zeros((ROPE, HEADS), jnp.bfloat16)

    def prefix(query, p):
        limit = pages[p]
        latent, rotary = query[:LAT], query[LAT:]
        keys = [
            jnp.concatenate(
                [gathered[:, :, 2 * lanes + tokens, p].reshape(256, 128) for lanes in range(4)], axis=1
            )
            for tokens in range(2)
        ]
        packed = gathered[:, :, p, PROMPTS].reshape(256, 128)
        scores = []
        for tokens in range(2):
            parts = [rotary, blank] if tokens == 0 else [blank, rotary]
            score = lax.dot_general(keys[tokens], latent, NN, preferred_element_type=jnp.float32)
            score = score + lax.dot_general(
                packed, jnp.concatenate(parts, axis=0), NN, preferred_element_type=jnp.float32
            )
            scores.append(jnp.where(page_of < limit, score * SCALE, BIG_NEGATIVE))
        return attend(scores, [lambda key=key: key for key in keys])

    returns = []
    for row in range(ROWS_DEV):
        peak, total, numerator = prefix(others[row], other_prompt[row])
        partial[row, :, :LAT] = numerator
        partial[row, :, LAT : LAT + 128] = peak
        partial[row, :, LAT + 128 :] = total
        back = remote(partial.at[row], arrived.at[row], c_send.at[2 + row], c_recv.at[2 + row], twin)
        back.start()
        returns.append(back)

    for row in range(ROWS_DEV):
        peak, total, numerator = prefix(queries[row], prompt[row])
        returns[row].wait_recv()
        m0, t0 = stats[row, 0], stats[row, 1]
        m1, t1 = arrived[row, :, LAT : LAT + 128], arrived[row, :, LAT + 128 :]
        top = jnp.maximum(jnp.maximum(peak, m0), m1)
        f, f0, f1 = jnp.exp(peak - top), jnp.exp(m0 - top), jnp.exp(m1 - top)
        whole = total * f + t0 * f0 + t1 * f1
        f, f0, f1 = f / whole, f0 / whole, f1 / whole
        for lanes in range(0, LAT, 128):
            part = slice(lanes, lanes + 128)
            summed = numerator[:, part] * f + numer[row, :, part] * f0 + arrived[row, :, part] * f1
            out[row, :, part] = summed.astype(out.dtype)

    @pl.loop(1, NEAR)
    def _(i):
        spread(i).wait_send()

    @pl.loop(1, Z)
    def _(i):
        z_out(i).wait_send()

    @pl.loop(1, TP)
    def _(i):
        t_out(i).wait_send()

    for copy in started + [trade, prompt_copy, query_copy] + returns:
        copy.wait_send()


def on_device(
    q_latent, page_pool, block_table, cache_len, prompt_of_row, prefix_cache, prefix_pages, owners
):
    anywhere = pl.BlockSpec(memory_space=pl.ANY)
    i32 = jnp.int32
    bf16, f32 = jnp.bfloat16, jnp.float32
    dma = pltpu.SemaphoreType.DMA
    return pl.pallas_call(
        kernel,
        out_shape=jax.ShapeDtypeStruct((ROWS_DEV, HEADS, LAT), bf16),
        in_specs=[anywhere] * 8,
        out_specs=pl.BlockSpec(memory_space=pltpu.VMEM),
        scratch_shapes=[
            pltpu.SMEM((ROWS_DEV, MAXP), i32),
            pltpu.SMEM((ROWS_DEV,), i32),
            pltpu.SMEM((ROWS_DEV,), i32),
            pltpu.SMEM((PROMPTS,), i32),
            pltpu.SMEM((PROMPTS,), i32),
            pltpu.VMEM((ROWS_DEV, WIDTH, HEADS), bf16),
            pltpu.VMEM((1, PAGE, WIDTH), bf16),
            pltpu.VMEM((Y, X, Z, POS, 16, 128), bf16),
            pltpu.VMEM((NEAR, 2, 16, 128), bf16),
            pltpu.VMEM((POS, 16, 128), bf16),
            pltpu.VMEM((POS, 16, 128), bf16),
            pltpu.VMEM((2, Z, 2, 16, 128), bf16),
            pltpu.VMEM((ROWS_DEV * MAXP, PAGE, WIDTH), bf16),
            pltpu.VMEM((ROWS_DEV, WIDTH, HEADS), bf16),
            pltpu.VMEM((ROWS_DEV,), i32),
            pltpu.SMEM((ROWS_DEV,), i32),
            pltpu.VMEM((ROWS_DEV, HEADS, LAT + 256), f32),
            pltpu.VMEM((ROWS_DEV, HEADS, LAT + 256), f32),
            pltpu.VMEM((ROWS_DEV, HEADS, LAT), f32),
            pltpu.VMEM((ROWS_DEV, 2, HEADS, 128), f32),
            dma((8,)), dma,
            dma((NEAR,)), dma((NEAR,)),
            dma((Z,)), dma((Z,)),
            dma((TP,)), dma((TP,)),
            dma((38,)), dma((38,)),
            dma((5,)), dma((5,)),
        ],
        compiler_params=pltpu.CompilerParams(
            collective_id=0, has_side_effects=True, vmem_limit_bytes=60 * 1024 * 1024
        ),
        cost_estimate=pl.CostEstimate(flops=1200000000, bytes_accessed=3000000, transcendentals=600000),
    )(
        block_table, cache_len, prompt_of_row, prefix_pages, owners,
        jnp.swapaxes(q_latent, 1, 2), prefix_cache, page_pool,
    )


def solution(mesh):
    placed = (
        P(("dp", "tp"), None, None),
        P(("dp", "tp"), None, None),
        P(("dp", "tp"), None),
        P(("dp", "tp")),
        P(("dp", "tp")),
        P("dp", "tp", None),
        P(),
        P(),
    )
    return jax.shard_map(
        on_device,
        mesh=mesh,
        in_specs=placed,
        out_specs=P(("dp", "tp"), None, None),
        check_vma=False,
    )
```

time: 506 us -> 61.6 us (0.12)
  waiting for transfers between devices: 456 us -> 0 us
  Pallas kernels: 0 us -> 59.8 us
  between operations: 19.2 us -> 0.01 us
  local copies, waits for them, and re-layouts: 20.6 us -> 1.67 us
  matrix products: 5.41 us -> 0 us
    psum x1 -> x0, waiting for transfers between devices: 344 us -> none  [broadcast(): return lax.psum(jnp.where(mine, x, jnp.zeros_like(x)), axis)]
    all_gather x1 -> x0, waiting for transfers between devices: 112 us -> none  [on_device(): piece = lax.all_gather(prefix, 'tp', axis=1, tiled=True)]
    pallas_call x0 -> x1, Pallas kernels: none -> 59.8 us  [on_device(): pl.pallas_call(kernel, out_shape=jax.ShapeDtypeStruct((ROWS_DEV, HEADS, L...]
    gather x4 -> x0, local copies, waits for them, and re-layouts: 10.7 us -> none  [the longest x2 5.04 us: private_step(): keys = page_pool[pages].reshape(rows_dev, span, width)]
    unnamed x19 -> x1, local copies, waits for them, and re-layouts: 7.16 us -> 1.67 us
    dot_general x6 -> x0, matrix products: 5.41 us -> none  [the longest x3 3.3 us: attend(): jnp.einsum('rht,rtv->rhv', weight.astype(jnp.bfloat16), values, preferred...]
  transfers between devices with their start and end apart: 2 -> 0, of which waited for: 2 -> 0; matrix products, arithmetic and copies ran while one was open for 2% -> 0% of each run, Pallas kernels for 0% -> 0%
where the time goes in v1:
time: 61.6 us; the launch traced here: 61.5 us
  Pallas kernels  59.8 us (97%)
  local copies, waits for them, and re-layouts  1.67 us (3%)
    pallas_call x1, Pallas kernels, on_device(): pl.pallas_call(kernel, out_shape=jax.ShapeDtypeStruct((ROWS_DEV, HEADS, L...  59.8 us
    unnamed x1, local copies, waits for them, and re-layouts  1.67 us

profile of v1, /device:TPU:1, one launch (start us, length us, event | category | flops | bytes accessed | tf_op | source)
XLA Modules:
  0.0 61.5 jit_solution(11417679444904335095)
XLA Ops:
  0.0 59.8 %shard_map.82 = bf16[2,128,512]{2,1,0:T(8,128)(2,1)} custom-call(s32[2,16]{1,0:T(2,128)} %table_hbm.1, s32[2]{0:T(128)} %length_hbm.1, s32[2]{0:T(128)} %prompt_hbm.1, s32[8]{0:T(128)} %pages_hbm.1, s32[8]{0:T(128)} %owners_hbm.1, bf16[2,576,128]{2,1,0:T(8,128)(2,1)} %bitcast.1, bf16[1,64,576]{2,1,0:T(8,128)(2,1)} %slot_hbm.1, bf16[32,64,576]{2,1,0:T(8,128)(2,1)} %pool_hbm.1), custom_call_target="tpu_custom_call" | custom-call | flops 1200000000 | bytes 3000000 | tf_op jit(solution)/shard_map/pallas_call | solution.py:352
  59.8 1.7 %copy.10 = bf16[2,128,512]{2,1,0:T(8,128)(2,1)} copy(bf16[2,128,512]{2,1,0:T(8,128)(2,1)} %shard_map.82) | data formatting | bytes 524288

commit v2 on v1

--- a/solution.py
+++ b/solution.py
@@ -240,9 +240,50 @@
 
     ay = Ring(lambda y, h: gathered.at[y, x, 4 * h : 4 * h + 4, 0:3], y_lo, at_y, 0, Y, 2)
     bx = Ring(lambda at, h: gathered.at[y_lo, at, 4 * h : 4 * h + 4, 3:6], x, at_x, 6, X, 2)
-    ax = Ring(lambda at, h: gathered.at[2 * h : 2 * h + 2, at, :, 0:3], x, at_x, 12, X, 2)
-    by = Ring(lambda y, h: gathered.at[y, 2 * h : 2 * h + 2, :, 3:6], y_lo, at_y, 18, Y, 2)
-    cz = Ring(lambda at, h: gathered.at[2 * h : 2 * h + 2, :, at, 6:9], z, at_z, 24, Z, 4)
+    class Slab:
+        def __init__(self, piece, place, device, first):
+            self.piece, self.place, self.device, self.first = piece, place, device, first
+
+        def copy(self, step, way, behind):
+            sign = 1 - 2 * way
+            origin = (self.place - sign * behind + 8) % 4
+            ref = self.piece(origin, pl.ds(0, Z) if step == 1 else pl.ds(4 * way, 4))
+            index = self.first + 2 * (step - 1) + way
+            return remote(ref, ref, r_send.at[index], r_recv.at[index], self.device(sign))
+
+        def begin(self):
+            for way in range(2):
+                copy = self.copy(1, way, 0)
+                copy.start()
+                started.append(copy)
+
+        def land(self):
+            for way in range(2):
+                self.copy(1, way, 1).wait_recv()
+                copy = self.copy(2, way, 1)
+                copy.start()
+                started.append(copy)
+
+        def finish(self):
+            for way in range(2):
+                self.copy(2, way, 2).wait_recv()
+
+    def slab_x(offset):
+        row = (y_lo + offset) % Y
+        return Slab(lambda at, zs: gathered.at[row, at, zs, 0:3], x, at_x, 26 + 4 * offset)
+
+    def slab_y(offset):
+        column = (x + offset) % X
+        return Slab(lambda at, zs: gathered.at[at, column, zs, 3:6], y_lo, at_y, 42 + 4 * offset)
+
+    slabs = [(slab_x(offset), slab_y(offset)) for offset in range(4)]
+
+    def each(action, *offsets):
+        for offset in offsets:
+            for slab in slabs[offset]:
+                action(slab)
+
+    cz = Ring(lambda at, h: gathered.at[2 * h : 2 * h + 2, :, at, 6:9], z, at_z, 12, Z, 4)
 
     @pl.loop(1, Z)
     def _(i):
@@ -250,6 +291,7 @@
 
     ay.begin()
     bx.begin()
+    each(Slab.begin, 0)
 
     @pl.loop(1, TP)
     def _(i):
@@ -260,24 +302,24 @@
     bx.land(1, 0)
     ay.land(1, 1)
     bx.land(1, 1)
+    each(Slab.begin, 3, 1)
     cz.land(1, 0)
     ay.land(2, 0)
-    ax.begin()
     bx.land(2, 0)
-    by.begin()
+    each(Slab.begin, 2)
     cz.land(1, 1)
+    each(Slab.land, 0)
     cz.land(2, 0)
-    ax.land(1, 0)
-    by.land(1, 0)
+    each(Slab.land, 3)
     cz.land(2, 1)
+    each(Slab.land, 1)
     cz.land(3, 0)
-    ax.land(1, 1)
-    by.land(1, 1)
+    each(Slab.land, 2)
     query_copy.wait_recv()
+    each(Slab.finish, 0, 3, 1)
     cz.land(3, 1)
     cz.land(4, 0)
-    ax.land(2, 0)
-    by.land(2, 0)
+    each(Slab.finish, 2)
 
     page_of = lax.broadcasted_iota(jnp.int32, (256, HEADS), 0) // 16
     blank = jnp.zeros((ROPE, HEADS), jnp.bfloat16)
@@ -379,7 +421,7 @@
             dma((NEAR,)), dma((NEAR,)),
             dma((Z,)), dma((Z,)),
             dma((TP,)), dma((TP,)),
-            dma((38,)), dma((38,)),
+            dma((58,)), dma((58,)),
             dma((5,)), dma((5,)),
         ],
         compiler_params=pltpu.CompilerParams(

time: 61.6 us -> 61 us (level)
  no operation moved by 1% of the time
where the time goes in v2:
time: 61 us; the launch traced here: 60.9 us
  Pallas kernels  59.2 us (97%)
  local copies, waits for them, and re-layouts  1.67 us (3%)
    pallas_call x1, Pallas kernels, on_device(): pl.pallas_call(kernel, out_shape=jax.ShapeDtypeStruct((ROWS_DEV, HEADS, L...  59.2 us
    unnamed x1, local copies, waits for them, and re-layouts  1.67 us

profile of v2, /device:TPU:1, one launch (start us, length us, event | category | flops | bytes accessed | tf_op | source)
XLA Modules:
  0.0 60.9 jit_solution(7168518391729584038)
XLA Ops:
  0.0 59.2 %shard_map.82 = bf16[2,128,512]{2,1,0:T(8,128)(2,1)} custom-call(s32[2,16]{1,0:T(2,128)} %table_hbm.1, s32[2]{0:T(128)} %length_hbm.1, s32[2]{0:T(128)} %prompt_hbm.1, s32[8]{0:T(128)} %pages_hbm.1, s32[8]{0:T(128)} %owners_hbm.1, bf16[2,576,128]{2,1,0:T(8,128)(2,1)} %bitcast.1, bf16[1,64,576]{2,1,0:T(8,128)(2,1)} %slot_hbm.1, bf16[32,64,576]{2,1,0:T(8,128)(2,1)} %pool_hbm.1), custom_call_target="tpu_custom_call" | custom-call | flops 1200000000 | bytes 3000000 | tf_op jit(solution)/shard_map/pallas_call | solution.py:394
  59.2 1.7 %copy.10 = bf16[2,128,512]{2,1,0:T(8,128)(2,1)} copy(bf16[2,128,512]{2,1,0:T(8,128)(2,1)} %shard_map.82) | data formatting | bytes 524288

commit v3 on v2

--- a/solution.py
+++ b/solution.py
@@ -48,6 +48,26 @@
     def at_z(step):
         return ((y_hi * Z + (z + step + Z) % Z) * 2 + core, tp)
 
+    barrier = pltpu.get_barrier_semaphore()
+
+    def near(i):
+        return y_hi * NEAR + (dp + i) % NEAR
+
+    partner = ((1 - y_hi) * NEAR + dp % NEAR, tp)
+
+    @pl.loop(1, NEAR)
+    def _(i):
+        pl.semaphore_signal(barrier, inc=1, device_id=(near(i), tp), device_id_type=MESH)
+
+    pl.semaphore_signal(barrier, inc=1, device_id=partner, device_id_type=MESH)
+
+    @pl.loop(1, TP)
+    def _(i):
+        pl.semaphore_signal(barrier, inc=1, device_id=(dp, (tp + i) % TP), device_id_type=MESH)
+
+    for step in (1, -1):
+        pl.semaphore_signal(barrier, inc=1, device_id=at_y(step), device_id_type=MESH)
+
     slot_copy, query_in, pool_copy, *small_copies = [
         pltpu.make_async_copy(source, target, local_sem.at[i])
         for i, (source, target) in enumerate((
@@ -58,26 +78,6 @@
     for copy in [slot_copy, query_in, pool_copy] + small_copies:
         copy.start()
 
-    barrier = pltpu.get_barrier_semaphore()
-
-    def near(i):
-        return y_hi * NEAR + (dp + i) % NEAR
-
-    partner = ((1 - y_hi) * NEAR + dp % NEAR, tp)
-
-    @pl.loop(1, NEAR)
-    def _(i):
-        pl.semaphore_signal(barrier, inc=1, device_id=(near(i), tp), device_id_type=MESH)
-
-    pl.semaphore_signal(barrier, inc=1, device_id=partner, device_id_type=MESH)
-
-    @pl.loop(1, TP)
-    def _(i):
-        pl.semaphore_signal(barrier, inc=1, device_id=(dp, (tp + i) % TP), device_id_type=MESH)
-
-    for step in (1, -1):
-        pl.semaphore_signal(barrier, inc=1, device_id=at_y(step), device_id_type=MESH)
-
     slot_copy.wait()
 
     for half in range(2):
@@ -121,45 +121,31 @@
     for copy in [query_in] + small_copies:
         copy.wait()
 
-    token = lax.broadcasted_iota(jnp.int32, (4 * PAGE, HEADS), 0)
+    token = lax.broadcasted_iota(jnp.int32, (MAXP * PAGE, HEADS), 0)
 
     def turned_wide(line):
         return jnp.transpose(jnp.broadcast_to(line, (HEADS, HEADS)))
 
-    def attend(scores, values):
-        peak = jnp.max(scores[0], axis=0, keepdims=True)
-        for score in scores[1:]:
-            peak = jnp.maximum(peak, jnp.max(score, axis=0, keepdims=True))
-        total = jnp.zeros((1, HEADS), jnp.float32)
-        numerator = jnp.zeros((HEADS, LAT), jnp.float32)
-        for score, value in zip(scores, values):
-            weight = jnp.exp(score - peak)
-            total = total + jnp.sum(weight, axis=0, keepdims=True)
-            numerator = numerator + lax.dot_general(
-                weight.astype(jnp.bfloat16), value(), TN, preferred_element_type=jnp.float32
-            )
+    def attend(score, values):
+        peak = jnp.max(score, axis=0, keepdims=True)
+        weight = jnp.exp(score - peak)
+        total = jnp.sum(weight, axis=0, keepdims=True)
+        numerator = lax.dot_general(
+            weight.astype(jnp.bfloat16), values, TN, preferred_element_type=jnp.float32
+        )
         return turned_wide(peak), turned_wide(total), numerator
 
     def private(row):
-        limit = length[row]
-
-        def block(number):
-            return jnp.concatenate([pool[table[row, 4 * number + i]] for i in range(4)], axis=0)
-
-        scores = []
-        for number in range(4):
-            score = lax.dot_general(block(number), queries[row], NN, preferred_element_type=jnp.float32)
-            scores.append(jnp.where(token + 256 * number < limit, score * SCALE, BIG_NEGATIVE))
-        peak, total, numerator = attend(
-            scores, [lambda number=number: block(number)[:, :LAT] for number in range(4)]
-        )
+        keys = jnp.concatenate([pool[table[row, i]] for i in range(MAXP)], axis=0)
+        score = lax.dot_general(keys, queries[row], NN, preferred_element_type=jnp.float32)
+        score = jnp.where(token < length[row], score * SCALE, BIG_NEGATIVE)
+        peak, total, numerator = attend(score, keys[:, :LAT])
         numer[row] = numerator
         stats[row, 0] = peak
         stats[row, 1] = total
 
     pool_copy.wait()
-    for row in range(ROWS_DEV):
-        private(row)
+    private(0)
 
     @pl.loop(1, NEAR)
     def _(i):
@@ -200,6 +186,7 @@
     def _(i):
         t_out(i).start()
 
+    private(1)
     prompt_copy.wait_recv()
     to_scalar = pltpu.make_async_copy(other_block, other_prompt, prompt_sem)
     to_scalar.start()
@@ -321,28 +308,30 @@
     cz.land(4, 0)
     each(Slab.finish, 2)
 
-    page_of = lax.broadcasted_iota(jnp.int32, (256, HEADS), 0) // 16
+    page_of = lax.broadcasted_iota(jnp.int32, (512, HEADS), 0) // 16 % TP
     blank = jnp.zeros((ROPE, HEADS), jnp.bfloat16)
 
     def prefix(query, p):
-        limit = pages[p]
         latent, rotary = query[:LAT], query[LAT:]
-        keys = [
-            jnp.concatenate(
-                [gathered[:, :, 2 * lanes + tokens, p].reshape(256, 128) for lanes in range(4)], axis=1
-            )
-            for tokens in range(2)
-        ]
+        keys = jnp.concatenate(
+            [
+                jnp.concatenate(
+                    [gathered[:, :, 2 * lanes + tokens, p].reshape(256, 128) for lanes in range(4)], axis=1
+                )
+                for tokens in range(2)
+            ],
+            axis=0,
+        )
         packed = gathered[:, :, p, PROMPTS].reshape(256, 128)
-        scores = []
-        for tokens in range(2):
-            parts = [rotary, blank] if tokens == 0 else [blank, rotary]
-            score = lax.dot_general(keys[tokens], latent, NN, preferred_element_type=jnp.float32)
-            score = score + lax.dot_general(
+        turned = [
+            lax.dot_general(
                 packed, jnp.concatenate(parts, axis=0), NN, preferred_element_type=jnp.float32
             )
-            scores.append(jnp.where(page_of < limit, score * SCALE, BIG_NEGATIVE))
-        return attend(scores, [lambda key=key: key for key in keys])
+            for parts in ([rotary, blank], [blank, rotary])
+        ]
+        score = lax.dot_general(keys, latent, NN, preferred_element_type=jnp.float32)
+        score = (score + jnp.concatenate(turned, axis=0)) * SCALE
+        return attend(jnp.where(page_of < pages[p], score, BIG_NEGATIVE), keys)
 
     returns = []
     for row in range(ROWS_DEV):

time: 61 us -> 61 us (level)
  no operation moved by 1% of the time
where the time goes in v3:
time: 61 us; the launch traced here: 60.8 us
  Pallas kernels  59.2 us (97%)
  local copies, waits for them, and re-layouts  1.67 us (3%)
    pallas_call x1, Pallas kernels, on_device(): pl.pallas_call(kernel, out_shape=jax.ShapeDtypeStruct((ROWS_DEV, HEADS, L...  59.2 us
    unnamed x1, local copies, waits for them, and re-layouts  1.67 us

profile of v3, /device:TPU:1, one launch (start us, length us, event | category | flops | bytes accessed | tf_op | source)
XLA Modules:
  0.0 60.8 jit_solution(10210648670648331845)
XLA Ops:
  0.0 59.2 %shard_map.82 = bf16[2,128,512]{2,1,0:T(8,128)(2,1)} custom-call(s32[2,16]{1,0:T(2,128)} %table_hbm.1, s32[2]{0:T(128)} %length_hbm.1, s32[2]{0:T(128)} %prompt_hbm.1, s32[8]{0:T(128)} %pages_hbm.1, s32[8]{0:T(128)} %owners_hbm.1, bf16[2,576,128]{2,1,0:T(8,128)(2,1)} %bitcast.1, bf16[1,64,576]{2,1,0:T(8,128)(2,1)} %slot_hbm.1, bf16[32,64,576]{2,1,0:T(8,128)(2,1)} %pool_hbm.1), custom_call_target="tpu_custom_call" | custom-call | flops 1200000000 | bytes 3000000 | tf_op jit(solution)/shard_map/pallas_call | solution.py:383
  59.2 1.7 %copy.10 = bf16[2,128,512]{2,1,0:T(8,128)(2,1)} copy(bf16[2,128,512]{2,1,0:T(8,128)(2,1)} %shard_map.82) | data formatting | bytes 524288

commit v4 on v3

--- a/solution.py
+++ b/solution.py
@@ -61,11 +61,9 @@
 
     pl.semaphore_signal(barrier, inc=1, device_id=partner, device_id_type=MESH)
 
-    @pl.loop(1, TP)
-    def _(i):
-        pl.semaphore_signal(barrier, inc=1, device_id=(dp, (tp + i) % TP), device_id_type=MESH)
-
     for step in (1, -1):
+        pl.semaphore_signal(barrier, inc=1, device_id=at_x(step), device_id_type=MESH)
+    for step in (1, -1, 2, -2):
         pl.semaphore_signal(barrier, inc=1, device_id=at_y(step), device_id_type=MESH)
 
     slot_copy, query_in, pool_copy, *small_copies = [
@@ -90,7 +88,7 @@
             staged[half, tile, 0] = slot[0, first : first + 16, 128 * lanes : 128 * lanes + 128]
             staged[half, tile, 1] = rotary
 
-    pl.semaphore_wait(barrier, NEAR - 1 + 1 + TP - 1 + 2)
+    pl.semaphore_wait(barrier, NEAR - 1 + 1 + 2 + 4)
 
     def remote(src, dst, send, recv, device):
         return pltpu.make_async_remote_copy(
@@ -146,6 +144,9 @@
 
     pool_copy.wait()
     private(0)
+    prompt_copy.wait_recv()
+    to_scalar = pltpu.make_async_copy(other_block, other_prompt, prompt_sem)
+    to_scalar.start()
 
     @pl.loop(1, NEAR)
     def _(i):
@@ -156,41 +157,34 @@
     picked[PROMPTS] = received[owners[z] % NEAR, 1]
     trade = remote(picked, traded, c_send.at[4], c_recv.at[4], partner)
     trade.start()
+    private(1)
     trade.wait_recv()
     for p in range(POS):
         owner = owners[p] if p < PROMPTS else owners[z]
         gathered[y_lo, x, z, p] = jnp.where(owner // NEAR == y_hi, picked[p], traded[p])
 
-    def z_out(i):
-        mine = gathered.at[y_lo, x, z, 0:6]
-        return remote(mine, mine, z_send.at[i], z_recv.at[i], at_z(i))
-
-    def z_in(i):
-        theirs = gathered.at[y_lo, x, (z - i + Z) % Z, 0:6]
-        return remote(theirs, theirs, z_send.at[i], z_recv.at[i], at_z(i))
-
-    def t_out(i):
-        mine = gathered.at[y_lo, x, z, 6:9]
-        return remote(mine, mine, t_send.at[i], t_recv.at[i], (dp, (tp + i) % TP))
-
-    def t_in(i):
-        source = (tp - i + TP) % TP
-        theirs = gathered.at[source // X, source % X, z, 6:9]
-        return remote(theirs, theirs, t_send.at[i], t_recv.at[i], (dp, (tp + i) % TP))
-
-    @pl.loop(1, Z)
-    def _(i):
-        z_out(i).start()
-
-    @pl.loop(1, TP)
-    def _(i):
-        t_out(i).start()
-
-    private(1)
-    prompt_copy.wait_recv()
-    to_scalar = pltpu.make_async_copy(other_block, other_prompt, prompt_sem)
-    to_scalar.start()
-    to_scalar.wait()
+    z_moves = (
+        (1, 0, 0, 6), (-1, 0, 0, 6), (2, 0, 0, 6), (-2, 0, 0, 6),
+        (2, -1, 0, 6), (-2, 1, 0, 6), (2, -2, 0, 3), (-2, 2, 3, 6),
+    )
+
+    def z_copy(number, arriving):
+        to, origin, low, high = z_moves[number]
+        at = (z + origin - (to if arriving else 0) + 2 * Z) % Z
+        ref = gathered.at[y_lo, x, at, low:high]
+        return remote(ref, ref, z_send.at[number], z_recv.at[number], at_z(to))
+
+    y_moves = ((1, 6, 9), (-1, 6, 9), (2, 6, 8), (-2, 8, 9))
+
+    def y_copy(number, arriving):
+        to, low, high = y_moves[number]
+        at = (y_lo - (to if arriving else 0) + Y) % Y
+        ref = gathered.at[at, x, z, low:high]
+        return remote(ref, ref, t_send.at[number], t_recv.at[number], at_y(to))
+
+    for number in range(4):
+        y_copy(number, False).start()
+        z_copy(number, False).start()
 
     started = []
 
@@ -271,20 +265,24 @@
                 action(slab)
 
     cz = Ring(lambda at, h: gathered.at[2 * h : 2 * h + 2, :, at, 6:9], z, at_z, 12, Z, 4)
-
-    @pl.loop(1, Z)
-    def _(i):
-        z_in(i).wait_recv()
-
+    cx = Ring(lambda at, h: gathered.at[2 * h : 2 * h + 2, at, z, 6:9], x, at_x, 58, X, 2)
+
+    for number in range(4):
+        y_copy(number, True).wait_recv()
+    cx.begin()
+    for number in range(4):
+        z_copy(number, True).wait_recv()
+        z_copy(number + 4, False).start()
+    cx.land(1, 0)
+    cx.land(1, 1)
+    cx.land(2, 0)
+    cz.begin()
+    for number in range(4, 8):
+        z_copy(number, True).wait_recv()
     ay.begin()
     bx.begin()
     each(Slab.begin, 0)
 
-    @pl.loop(1, TP)
-    def _(i):
-        t_in(i).wait_recv()
-
-    cz.begin()
     ay.land(1, 0)
     bx.land(1, 0)
     ay.land(1, 1)
@@ -333,6 +331,7 @@
         score = (score + jnp.concatenate(turned, axis=0)) * SCALE
         return attend(jnp.where(page_of < pages[p], score, BIG_NEGATIVE), keys)
 
+    to_scalar.wait()
     returns = []
     for row in range(ROWS_DEV):
         peak, total, numerator = prefix(others[row], other_prompt[row])
@@ -361,14 +360,10 @@
     def _(i):
         spread(i).wait_send()
 
-    @pl.loop(1, Z)
-    def _(i):
-        z_out(i).wait_send()
-
-    @pl.loop(1, TP)
-    def _(i):
-        t_out(i).wait_send()
-
+    for number in range(8):
+        z_copy(number, False).wait_send()
+    for number in range(4):
+        y_copy(number, False).wait_send()
     for copy in started + [trade, prompt_copy, query_copy] + returns:
         copy.wait_send()
 
@@ -409,8 +404,8 @@
             dma((8,)), dma,
             dma((NEAR,)), dma((NEAR,)),
             dma((Z,)), dma((Z,)),
-            dma((TP,)), dma((TP,)),
-            dma((58,)), dma((58,)),
+            dma((4,)), dma((4,)),
+            dma((64,)), dma((64,)),
             dma((5,)), dma((5,)),
         ],
         compiler_params=pltpu.CompilerParams(

time: 61 us -> 64 us (1.049)
  Pallas kernels: 59.2 us -> 62.2 us
    pallas_call x1, Pallas kernels: 59.2 us -> 62.2 us  [on_device(): pl.pallas_call(kernel, out_shape=jax.ShapeDtypeStruct((ROWS_DEV, HEADS, L...]
where the time goes in v4:
time: 64 us; the launch traced here: 63.8 us
  Pallas kernels  62.2 us (97%)
  local copies, waits for them, and re-layouts  1.67 us (3%)
    pallas_call x1, Pallas kernels, on_device(): pl.pallas_call(kernel, out_shape=jax.ShapeDtypeStruct((ROWS_DEV, HEADS, L...  62.2 us
    unnamed x1, local copies, waits for them, and re-layouts  1.67 us

profile of v4, /device:TPU:1, one launch (start us, length us, event | category | flops | bytes accessed | tf_op | source)
XLA Modules:
  0.0 63.8 jit_solution(17042406390024061474)
XLA Ops:
  0.0 62.2 %shard_map.82 = bf16[2,128,512]{2,1,0:T(8,128)(2,1)} custom-call(s32[2,16]{1,0:T(2,128)} %table_hbm.1, s32[2]{0:T(128)} %length_hbm.1, s32[2]{0:T(128)} %prompt_hbm.1, s32[8]{0:T(128)} %pages_hbm.1, s32[8]{0:T(128)} %owners_hbm.1, bf16[2,576,128]{2,1,0:T(8,128)(2,1)} %bitcast.1, bf16[1,64,576]{2,1,0:T(8,128)(2,1)} %slot_hbm.1, bf16[32,64,576]{2,1,0:T(8,128)(2,1)} %pool_hbm.1), custom_call_target="tpu_custom_call" | custom-call | flops 1200000000 | bytes 3000000 | tf_op jit(solution)/shard_map/pallas_call | solution.py:378
  62.2 1.7 %copy.10 = bf16[2,128,512]{2,1,0:T(8,128)(2,1)} copy(bf16[2,128,512]{2,1,0:T(8,128)(2,1)} %shard_map.82) | data formatting | bytes 524288

commit v5 on v3

--- a/solution.py
+++ b/solution.py
@@ -23,6 +23,14 @@
 NN = (((1,), (0,)), ((), ()))
 
 
+def each_of(first, end):
+    def run(body):
+        for i in range(first, end):
+            body(i)
+
+    return run
+
+
 def kernel(
     table_hbm, length_hbm, prompt_hbm, pages_hbm, owners_hbm, queries_hbm, slot_hbm, pool_hbm, out,
     table, length, prompt, pages, owners, queries, slot, gathered, received, picked, traded, staged, pool, others, other_block,
@@ -55,13 +63,13 @@
 
     partner = ((1 - y_hi) * NEAR + dp % NEAR, tp)
 
-    @pl.loop(1, NEAR)
+    @each_of(1, NEAR)
     def _(i):
         pl.semaphore_signal(barrier, inc=1, device_id=(near(i), tp), device_id_type=MESH)
 
     pl.semaphore_signal(barrier, inc=1, device_id=partner, device_id_type=MESH)
 
-    @pl.loop(1, TP)
+    @each_of(1, TP)
     def _(i):
         pl.semaphore_signal(barrier, inc=1, device_id=(dp, (tp + i) % TP), device_id_type=MESH)
 
@@ -109,7 +117,7 @@
             staged.at[0, 0], received.at[source], p1_send.at[i], p1_recv.at[i], (near(i), tp)
         )
 
-    @pl.loop(1, NEAR)
+    @each_of(1, NEAR)
     def _(i):
         spread(i).start()
 
@@ -146,8 +154,11 @@
 
     pool_copy.wait()
     private(0)
-
-    @pl.loop(1, NEAR)
+    prompt_copy.wait_recv()
+    to_scalar = pltpu.make_async_copy(other_block, other_prompt, prompt_sem)
+    to_scalar.start()
+
+    @each_of(1, NEAR)
     def _(i):
         spread_in(i).wait_recv()
 
@@ -178,20 +189,15 @@
         theirs = gathered.at[source // X, source % X, z, 6:9]
         return remote(theirs, theirs, t_send.at[i], t_recv.at[i], (dp, (tp + i) % TP))
 
-    @pl.loop(1, Z)
+    @each_of(1, Z)
     def _(i):
         z_out(i).start()
 
-    @pl.loop(1, TP)
+    @each_of(1, TP)
     def _(i):
         t_out(i).start()
 
     private(1)
-    prompt_copy.wait_recv()
-    to_scalar = pltpu.make_async_copy(other_block, other_prompt, prompt_sem)
-    to_scalar.start()
-    to_scalar.wait()
-
     started = []
 
     class Ring:
@@ -272,7 +278,7 @@
 
     cz = Ring(lambda at, h: gathered.at[2 * h : 2 * h + 2, :, at, 6:9], z, at_z, 12, Z, 4)
 
-    @pl.loop(1, Z)
+    @each_of(1, Z)
     def _(i):
         z_in(i).wait_recv()
 
@@ -280,7 +286,7 @@
     bx.begin()
     each(Slab.begin, 0)
 
-    @pl.loop(1, TP)
+    @each_of(1, TP)
     def _(i):
         t_in(i).wait_recv()
 
@@ -333,6 +339,7 @@
         score = (score + jnp.concatenate(turned, axis=0)) * SCALE
         return attend(jnp.where(page_of < pages[p], score, BIG_NEGATIVE), keys)
 
+    to_scalar.wait()
     returns = []
     for row in range(ROWS_DEV):
         peak, total, numerator = prefix(others[row], other_prompt[row])
@@ -357,15 +364,15 @@
             summed = numerator[:, part] * f + numer[row, :, part] * f0 + arrived[row, :, part] * f1
             out[row, :, part] = summed.astype(out.dtype)
 
-    @pl.loop(1, NEAR)
+    @each_of(1, NEAR)
     def _(i):
         spread(i).wait_send()
 
-    @pl.loop(1, Z)
+    @each_of(1, Z)
     def _(i):
         z_out(i).wait_send()
 
-    @pl.loop(1, TP)
+    @each_of(1, TP)
     def _(i):
         t_out(i).wait_send()
 

time: 61 us -> 60.7 us (level)
  no operation moved by 1% of the time
where the time goes in v5:
time: 60.7 us; the launch traced here: 60.5 us
  Pallas kernels  58.8 us (97%)
  local copies, waits for them, and re-layouts  1.67 us (3%)
    pallas_call x1, Pallas kernels, on_device(): pl.pallas_call(kernel, out_shape=jax.ShapeDtypeStruct((ROWS_DEV, HEADS, L...  58.8 us
    unnamed x1, local copies, waits for them, and re-layouts  1.67 us

profile of v5, /device:TPU:1, one launch (start us, length us, event | category | flops | bytes accessed | tf_op | source)
XLA Modules:
  0.0 60.5 jit_solution(8961878773519090909)
XLA Ops:
  0.0 58.8 %shard_map.82 = bf16[2,128,512]{2,1,0:T(8,128)(2,1)} custom-call(s32[2,16]{1,0:T(2,128)} %table_hbm.1, s32[2]{0:T(128)} %length_hbm.1, s32[2]{0:T(128)} %prompt_hbm.1, s32[8]{0:T(128)} %pages_hbm.1, s32[8]{0:T(128)} %owners_hbm.1, bf16[2,576,128]{2,1,0:T(8,128)(2,1)} %bitcast.1, bf16[1,64,576]{2,1,0:T(8,128)(2,1)} %slot_hbm.1, bf16[32,64,576]{2,1,0:T(8,128)(2,1)} %pool_hbm.1), custom_call_target="tpu_custom_call" | custom-call | flops 1200000000 | bytes 3000000 | tf_op jit(solution)/shard_map/pallas_call | solution.py:390
  58.8 1.7 %copy.10 = bf16[2,128,512]{2,1,0:T(8,128)(2,1)} copy(bf16[2,128,512]{2,1,0:T(8,128)(2,1)} %shard_map.82) | data formatting | bytes 524288

commit v6 on v5

--- a/solution.py
+++ b/solution.py
@@ -15,6 +15,9 @@
 ROWS_DEV = 2
 X, Y, Z, DP, TP = 4, 4, 8, 32, 16
 NEAR = 2 * Z
+NEAR_ORDER = sorted(range(1, NEAR), key=lambda i: -min(i, NEAR - i))
+Z_ORDER = sorted(range(1, Z), key=lambda i: -min(i, Z - i))
+TP_ORDER = [4 * dy + dx for dx in (2, 1, 3, 0) for dy in (2, 1, 3, 0)][:-1]
 POS = PROMPTS + 1
 SCALE = 192.0 ** (-0.5)
 BIG_NEGATIVE = -1e30
@@ -23,18 +26,18 @@
 NN = (((1,), (0,)), ((), ()))
 
 
-def each_of(first, end):
+def each_of(numbers):
     def run(body):
-        for i in range(first, end):
+        for i in numbers:
             body(i)
 
     return run
 
 
 def kernel(
-    table_hbm, length_hbm, prompt_hbm, pages_hbm, owners_hbm, queries_hbm, slot_hbm, pool_hbm, out,
+    table_hbm, length_hbm, prompt_hbm, pages_hbm, owners_hbm, queries_hbm, slot_hbm, pool_hbm, out_hbm,
     table, length, prompt, pages, owners, queries, slot, gathered, received, picked, traded, staged, pool, others, other_block,
-    other_prompt, partial, arrived, numer, stats,
+    other_prompt, partial, arrived, numer, stats, out,
     local_sem, prompt_sem, p1_send, p1_recv, z_send, z_recv, t_send, t_recv, r_send, r_recv, c_send, c_recv,
 ):
     dp = lax.axis_index("dp")
@@ -61,17 +64,20 @@
     def near(i):
         return y_hi * NEAR + (dp + i) % NEAR
 
+    def group(i, sign):
+        return (y_lo + sign * (i // X) + Y) % Y * X + (x + sign * (i % X) + X) % X
+
     partner = ((1 - y_hi) * NEAR + dp % NEAR, tp)
 
-    @each_of(1, NEAR)
+    @each_of(NEAR_ORDER)
     def _(i):
         pl.semaphore_signal(barrier, inc=1, device_id=(near(i), tp), device_id_type=MESH)
 
     pl.semaphore_signal(barrier, inc=1, device_id=partner, device_id_type=MESH)
 
-    @each_of(1, TP)
-    def _(i):
-        pl.semaphore_signal(barrier, inc=1, device_id=(dp, (tp + i) % TP), device_id_type=MESH)
+    @each_of(TP_ORDER)
+    def _(i):
+        pl.semaphore_signal(barrier, inc=1, device_id=(dp, group(i, 1)), device_id_type=MESH)
 
     for step in (1, -1):
         pl.semaphore_signal(barrier, inc=1, device_id=at_y(step), device_id_type=MESH)
@@ -117,7 +123,7 @@
             staged.at[0, 0], received.at[source], p1_send.at[i], p1_recv.at[i], (near(i), tp)
         )
 
-    @each_of(1, NEAR)
+    @each_of(NEAR_ORDER)
     def _(i):
         spread(i).start()
 
@@ -158,7 +164,7 @@
     to_scalar = pltpu.make_async_copy(other_block, other_prompt, prompt_sem)
     to_scalar.start()
 
-    @each_of(1, NEAR)
+    @each_of(NEAR_ORDER)
     def _(i):
         spread_in(i).wait_recv()
 
@@ -182,18 +188,18 @@
 
     def t_out(i):
         mine = gathered.at[y_lo, x, z, 6:9]
-        return remote(mine, mine, t_send.at[i], t_recv.at[i], (dp, (tp + i) % TP))
+        return remote(mine, mine, t_send.at[i], t_recv.at[i], (dp, group(i, 1)))
 
     def t_in(i):
-        source = (tp - i + TP) % TP
+        source = group(i, -1)
         theirs = gathered.at[source // X, source % X, z, 6:9]
-        return remote(theirs, theirs, t_send.at[i], t_recv.at[i], (dp, (tp + i) % TP))
-
-    @each_of(1, Z)
+        return remote(theirs, theirs, t_send.at[i], t_recv.at[i], (dp, group(i, 1)))
+
+    @each_of(Z_ORDER)
     def _(i):
         z_out(i).start()
 
-    @each_of(1, TP)
+    @each_of(TP_ORDER)
     def _(i):
         t_out(i).start()
 
@@ -278,7 +284,7 @@
 
     cz = Ring(lambda at, h: gathered.at[2 * h : 2 * h + 2, :, at, 6:9], z, at_z, 12, Z, 4)
 
-    @each_of(1, Z)
+    @each_of(Z_ORDER)
     def _(i):
         z_in(i).wait_recv()
 
@@ -286,7 +292,7 @@
     bx.begin()
     each(Slab.begin, 0)
 
-    @each_of(1, TP)
+    @each_of(TP_ORDER)
     def _(i):
         t_in(i).wait_recv()
 
@@ -341,6 +347,7 @@
 
     to_scalar.wait()
     returns = []
+    results = []
     for row in range(ROWS_DEV):
         peak, total, numerator = prefix(others[row], other_prompt[row])
         partial[row, :, :LAT] = numerator
@@ -363,21 +370,26 @@
             part = slice(lanes, lanes + 128)
             summed = numerator[:, part] * f + numer[row, :, part] * f0 + arrived[row, :, part] * f1
             out[row, :, part] = summed.astype(out.dtype)
-
-    @each_of(1, NEAR)
+        result = pltpu.make_async_copy(out.at[row], out_hbm.at[row], local_sem.at[8 + row])
+        result.start()
+        results.append(result)
+
+    @each_of(NEAR_ORDER)
     def _(i):
         spread(i).wait_send()
 
-    @each_of(1, Z)
+    @each_of(Z_ORDER)
     def _(i):
         z_out(i).wait_send()
 
-    @each_of(1, TP)
+    @each_of(TP_ORDER)
     def _(i):
         t_out(i).wait_send()
 
     for copy in started + [trade, prompt_copy, query_copy] + returns:
         copy.wait_send()
+    for result in results:
+        result.wait()
 
 
 def on_device(
@@ -391,7 +403,7 @@
         kernel,
         out_shape=jax.ShapeDtypeStruct((ROWS_DEV, HEADS, LAT), bf16),
         in_specs=[anywhere] * 8,
-        out_specs=pl.BlockSpec(memory_space=pltpu.VMEM),
+        out_specs=anywhere,
         scratch_shapes=[
             pltpu.SMEM((ROWS_DEV, MAXP), i32),
             pltpu.SMEM((ROWS_DEV,), i32),
@@ -413,7 +425,8 @@
             pltpu.VMEM((ROWS_DEV, HEADS, LAT + 256), f32),
             pltpu.VMEM((ROWS_DEV, HEADS, LAT), f32),
             pltpu.VMEM((ROWS_DEV, 2, HEADS, 128), f32),
-            dma((8,)), dma,
+            pltpu.VMEM((ROWS_DEV, HEADS, LAT), bf16),
+            dma((10,)), dma,
             dma((NEAR,)), dma((NEAR,)),
             dma((Z,)), dma((Z,)),
             dma((TP,)), dma((TP,)),

time: 60.7 us -> 59.5 us (0.980)
  Pallas kernels: 58.8 us -> 57.6 us
    pallas_call x1, Pallas kernels: 58.8 us -> 57.6 us  [on_device(): pl.pallas_call(kernel, out_shape=jax.ShapeDtypeStruct((ROWS_DEV, HEADS, L...]
where the time goes in v6:
time: 59.5 us; the launch traced here: 59.3 us
  Pallas kernels  57.6 us (97%)
  local copies, waits for them, and re-layouts  1.67 us (3%)
    pallas_call x1, Pallas kernels, on_device(): pl.pallas_call(kernel, out_shape=jax.ShapeDtypeStruct((ROWS_DEV, HEADS, L...  57.6 us
    unnamed x1, local copies, waits for them, and re-layouts  1.67 us

profile of v6, /device:TPU:1, one launch (start us, length us, event | category | flops | bytes accessed | tf_op | source)
XLA Modules:
  0.0 59.3 jit_solution(3473308686897840287)
XLA Ops:
  0.0 57.6 %shard_map.82 = bf16[2,128,512]{2,1,0:T(8,128)(2,1)} custom-call(s32[2,16]{1,0:T(2,128)} %table_hbm.1, s32[2]{0:T(128)} %length_hbm.1, s32[2]{0:T(128)} %prompt_hbm.1, s32[8]{0:T(128)} %pages_hbm.1, s32[8]{0:T(128)} %owners_hbm.1, bf16[2,576,128]{2,1,0:T(8,128)(2,1)} %bitcast.1, bf16[1,64,576]{2,1,0:T(8,128)(2,1)} %slot_hbm.1, bf16[32,64,576]{2,1,0:T(8,128)(2,1)} %pool_hbm.1), custom_call_target="tpu_custom_call" | custom-call | flops 1200000000 | bytes 3000000 | tf_op jit(solution)/shard_map/pallas_call | solution.py:402
  57.6 1.7 %copy.10 = bf16[2,128,512]{2,1,0:T(8,128)(2,1)} copy(bf16[2,128,512]{2,1,0:T(8,128)(2,1)} %shard_map.82) | data formatting | bytes 524288

commit v7 on v6

--- a/solution.py
+++ b/solution.py
@@ -64,8 +64,10 @@
     def near(i):
         return y_hi * NEAR + (dp + i) % NEAR
 
-    def group(i, sign):
-        return (y_lo + sign * (i // X) + Y) % Y * X + (x + sign * (i % X) + X) % X
+    def peer(i, sign):
+        dy = (0, 1, 2, -1)[i // X]
+        y = (y_hi * Y + y_lo + sign * dy + 2 * Y) % (2 * Y)
+        return (((y // Y) * Z + z) * 2 + core, y % Y * X + (x + sign * (i % X) + X) % X)
 
     partner = ((1 - y_hi) * NEAR + dp % NEAR, tp)
 
@@ -77,10 +79,7 @@
 
     @each_of(TP_ORDER)
     def _(i):
-        pl.semaphore_signal(barrier, inc=1, device_id=(dp, group(i, 1)), device_id_type=MESH)
-
-    for step in (1, -1):
-        pl.semaphore_signal(barrier, inc=1, device_id=at_y(step), device_id_type=MESH)
+        pl.semaphore_signal(barrier, inc=1, device_id=peer(i, -1), device_id_type=MESH)
 
     slot_copy, query_in, pool_copy, *small_copies = [
         pltpu.make_async_copy(source, target, local_sem.at[i])
@@ -104,7 +103,7 @@
             staged[half, tile, 0] = slot[0, first : first + 16, 128 * lanes : 128 * lanes + 128]
             staged[half, tile, 1] = rotary
 
-    pl.semaphore_wait(barrier, NEAR - 1 + 1 + TP - 1 + 2)
+    pl.semaphore_wait(barrier, NEAR - 1 + 1 + TP - 1)
 
     def remote(src, dst, send, recv, device):
         return pltpu.make_async_remote_copy(
@@ -188,12 +187,12 @@
 
     def t_out(i):
         mine = gathered.at[y_lo, x, z, 6:9]
-        return remote(mine, mine, t_send.at[i], t_recv.at[i], (dp, group(i, 1)))
+        return remote(mine, mine, t_send.at[i], t_recv.at[i], peer(i, 1))
 
     def t_in(i):
-        source = group(i, -1)
+        source = peer(i, -1)[1]
         theirs = gathered.at[source // X, source % X, z, 6:9]
-        return remote(theirs, theirs, t_send.at[i], t_recv.at[i], (dp, group(i, 1)))
+        return remote(theirs, theirs, t_send.at[i], t_recv.at[i], peer(i, 1))
 
     @each_of(Z_ORDER)
     def _(i):
@@ -284,6 +283,11 @@
 
     cz = Ring(lambda at, h: gathered.at[2 * h : 2 * h + 2, :, at, 6:9], z, at_z, 12, Z, 4)
 
+    @each_of(TP_ORDER)
+    def _(i):
+        t_in(i).wait_recv()
+
+    cz.begin()
     @each_of(Z_ORDER)
     def _(i):
         z_in(i).wait_recv()
@@ -292,11 +296,6 @@
     bx.begin()
     each(Slab.begin, 0)
 
-    @each_of(TP_ORDER)
-    def _(i):
-        t_in(i).wait_recv()
-
-    cz.begin()
     ay.land(1, 0)
     bx.land(1, 0)
     ay.land(1, 1)

time: 59.5 us -> 59.7 us (level)
  no operation moved by 1% of the time
where the time goes in v7:
time: 59.7 us; the launch traced here: 59.6 us
  Pallas kernels  57.9 us (97%)
  local copies, waits for them, and re-layouts  1.67 us (3%)
    pallas_call x1, Pallas kernels, on_device(): pl.pallas_call(kernel, out_shape=jax.ShapeDtypeStruct((ROWS_DEV, HEADS, L...  57.9 us
    unnamed x1, local copies, waits for them, and re-layouts  1.67 us

profile of v7, /device:TPU:1, one launch (start us, length us, event | category | flops | bytes accessed | tf_op | source)
XLA Modules:
  0.0 59.6 jit_solution(17387295217657170782)
XLA Ops:
  0.0 57.9 %shard_map.82 = bf16[2,128,512]{2,1,0:T(8,128)(2,1)} custom-call(s32[2,16]{1,0:T(2,128)} %table_hbm.1, s32[2]{0:T(128)} %length_hbm.1, s32[2]{0:T(128)} %prompt_hbm.1, s32[8]{0:T(128)} %pages_hbm.1, s32[8]{0:T(128)} %owners_hbm.1, bf16[2,576,128]{2,1,0:T(8,128)(2,1)} %bitcast.1, bf16[1,64,576]{2,1,0:T(8,128)(2,1)} %slot_hbm.1, bf16[32,64,576]{2,1,0:T(8,128)(2,1)} %pool_hbm.1), custom_call_target="tpu_custom_call" | custom-call | flops 1200000000 | bytes 3000000 | tf_op jit(solution)/shard_map/pallas_call | solution.py:401
  57.9 1.7 %copy.10 = bf16[2,128,512]{2,1,0:T(8,128)(2,1)} copy(bf16[2,128,512]{2,1,0:T(8,128)(2,1)} %shard_map.82) | data formatting | bytes 524288

commit v8 on v7

--- a/solution.py
+++ b/solution.py
@@ -16,7 +16,7 @@
 X, Y, Z, DP, TP = 4, 4, 8, 32, 16
 NEAR = 2 * Z
 NEAR_ORDER = sorted(range(1, NEAR), key=lambda i: -min(i, NEAR - i))
-Z_ORDER = sorted(range(1, Z), key=lambda i: -min(i, Z - i))
+Z_ORDER = (3, 5, 2, 6, 1, 7)
 TP_ORDER = [4 * dy + dx for dx in (2, 1, 3, 0) for dy in (2, 1, 3, 0)][:-1]
 POS = PROMPTS + 1
 SCALE = 192.0 ** (-0.5)
@@ -185,6 +185,12 @@
         theirs = gathered.at[y_lo, x, (z - i + Z) % Z, 0:6]
         return remote(theirs, theirs, z_send.at[i], z_recv.at[i], at_z(i))
 
+    def z_pass(sign, arriving):
+        origin = (z - (4 if arriving else 3) * sign + Z) % Z
+        low, index = (0, 4) if sign == 1 else (3, 0)
+        ref = gathered.at[y_lo, x, origin, low : low + 3]
+        return remote(ref, ref, z_send.at[index], z_recv.at[index], at_z(sign))
+
     def t_out(i):
         mine = gathered.at[y_lo, x, z, 6:9]
         return remote(mine, mine, t_send.at[i], t_recv.at[i], peer(i, 1))
@@ -283,28 +289,33 @@
 
     cz = Ring(lambda at, h: gathered.at[2 * h : 2 * h + 2, :, at, 6:9], z, at_z, 12, Z, 4)
 
-    @each_of(TP_ORDER)
-    def _(i):
-        t_in(i).wait_recv()
-
-    cz.begin()
     @each_of(Z_ORDER)
     def _(i):
         z_in(i).wait_recv()
+        if i in (3, 5):
+            z_pass(4 - i, False).start()
+
+    for sign in (1, -1):
+        z_pass(sign, True).wait_recv()
 
     ay.begin()
     bx.begin()
     each(Slab.begin, 0)
 
+    @each_of(TP_ORDER)
+    def _(i):
+        t_in(i).wait_recv()
+
+    cz.begin()
     ay.land(1, 0)
     bx.land(1, 0)
     ay.land(1, 1)
     bx.land(1, 1)
     each(Slab.begin, 3, 1)
-    cz.land(1, 0)
     ay.land(2, 0)
     bx.land(2, 0)
     each(Slab.begin, 2)
+    cz.land(1, 0)
     cz.land(1, 1)
     each(Slab.land, 0)
     cz.land(2, 0)
@@ -380,6 +391,9 @@
     @each_of(Z_ORDER)
     def _(i):
         z_out(i).wait_send()
+
+    for sign in (1, -1):
+        z_pass(sign, False).wait_send()
 
     @each_of(TP_ORDER)
     def _(i):

time: 59.7 us -> 63.3 us (1.060)
  Pallas kernels: 57.9 us -> 61.4 us
    pallas_call x1, Pallas kernels: 57.9 us -> 61.4 us  [on_device(): pl.pallas_call(kernel, out_shape=jax.ShapeDtypeStruct((ROWS_DEV, HEADS, L...]
where the time goes in v8:
time: 63.3 us; the launch traced here: 63.1 us
  Pallas kernels  61.4 us (97%)
  local copies, waits for them, and re-layouts  1.67 us (3%)
    pallas_call x1, Pallas kernels, on_device(): pl.pallas_call(kernel, out_shape=jax.ShapeDtypeStruct((ROWS_DEV, HEADS, L...  61.4 us
    unnamed x1, local copies, waits for them, and re-layouts  1.67 us

profile of v8, /device:TPU:1, one launch (start us, length us, event | category | flops | bytes accessed | tf_op | source)
XLA Modules:
  0.0 63.1 jit_solution(2112817171588851841)
XLA Ops:
  0.0 61.4 %shard_map.82 = bf16[2,128,512]{2,1,0:T(8,128)(2,1)} custom-call(s32[2,16]{1,0:T(2,128)} %table_hbm.1, s32[2]{0:T(128)} %length_hbm.1, s32[2]{0:T(128)} %prompt_hbm.1, s32[8]{0:T(128)} %pages_hbm.1, s32[8]{0:T(128)} %owners_hbm.1, bf16[2,576,128]{2,1,0:T(8,128)(2,1)} %bitcast.1, bf16[1,64,576]{2,1,0:T(8,128)(2,1)} %slot_hbm.1, bf16[32,64,576]{2,1,0:T(8,128)(2,1)} %pool_hbm.1), custom_call_target="tpu_custom_call" | custom-call | flops 1200000000 | bytes 3000000 | tf_op jit(solution)/shard_map/pallas_call | solution.py:415
  61.4 1.7 %copy.10 = bf16[2,128,512]{2,1,0:T(8,128)(2,1)} copy(bf16[2,128,512]{2,1,0:T(8,128)(2,1)} %shard_map.82) | data formatting | bytes 524288

commit v9 on v7

--- a/solution.py
+++ b/solution.py
@@ -296,17 +296,17 @@
     bx.begin()
     each(Slab.begin, 0)
 
+    cz.land(1, 0)
     ay.land(1, 0)
     bx.land(1, 0)
     ay.land(1, 1)
     bx.land(1, 1)
     each(Slab.begin, 3, 1)
-    cz.land(1, 0)
+    cz.land(1, 1)
+    each(Slab.land, 0)
     ay.land(2, 0)
     bx.land(2, 0)
     each(Slab.begin, 2)
-    cz.land(1, 1)
-    each(Slab.land, 0)
     cz.land(2, 0)
     each(Slab.land, 3)
     cz.land(2, 1)

time: 59.7 us -> 59.9 us (level)
  no operation moved by 1% of the time
where the time goes in v9:
time: 59.9 us; the launch traced here: 59.7 us
  Pallas kernels  58 us (97%)
  local copies, waits for them, and re-layouts  1.67 us (3%)
    pallas_call x1, Pallas kernels, on_device(): pl.pallas_call(kernel, out_shape=jax.ShapeDtypeStruct((ROWS_DEV, HEADS, L...  58 us
    unnamed x1, local copies, waits for them, and re-layouts  1.67 us

profile of v9, /device:TPU:1, one launch (start us, length us, event | category | flops | bytes accessed | tf_op | source)
XLA Modules:
  0.0 59.7 jit_solution(598123182636578331)
XLA Ops:
  0.0 58.0 %shard_map.82 = bf16[2,128,512]{2,1,0:T(8,128)(2,1)} custom-call(s32[2,16]{1,0:T(2,128)} %table_hbm.1, s32[2]{0:T(128)} %length_hbm.1, s32[2]{0:T(128)} %prompt_hbm.1, s32[8]{0:T(128)} %pages_hbm.1, s32[8]{0:T(128)} %owners_hbm.1, bf16[2,576,128]{2,1,0:T(8,128)(2,1)} %bitcast.1, bf16[1,64,576]{2,1,0:T(8,128)(2,1)} %slot_hbm.1, bf16[32,64,576]{2,1,0:T(8,128)(2,1)} %pool_hbm.1), custom_call_target="tpu_custom_call" | custom-call | flops 1200000000 | bytes 3000000 | tf_op jit(solution)/shard_map/pallas_call | solution.py:401
  58.0 1.7 %copy.10 = bf16[2,128,512]{2,1,0:T(8,128)(2,1)} copy(bf16[2,128,512]{2,1,0:T(8,128)(2,1)} %shard_map.82) | data formatting | bytes 524288
